TPU v7x, 256 devices: a whole 4x4x8 slice. The times are simulated.
256 devices in a mesh: section: 16 (over z_lo, x, core), expert: 16 (over y, z_hi).
Axes of the slice: x: 4, y: 4, z: 8 (z_hi: 4, z_lo: 2; z = z_hi * 2 + z_lo), core: 2. Of those that a mesh axis runs over, the one named last changes fastest.
Arguments:
- handoff: bfloat16 [16, 2048, 2560], P('section', 'expert'), may hold values from -6 to 6
- grad_handoff: bfloat16 [16, 2048, 2560], P('section', 'expert'), may hold values from -6 to 6
- parked: bfloat16 [16, 2048, 2560], P('section', 'expert'), may hold values from -6 to 6
- ids_fwd: int32 [16, 2048, 2], P('section', 'expert'), may hold values from 0 to 7, all different within a row; in each aligned block of 128 rows (0 to 127, 128 to 255, ..., all dimensions but the last counted through in order) at most 48 rows name the same one
- gates_fwd: float32 [16, 2048, 2], P('section', 'expert'), may hold values from 0.2 to 1
- ids_bwd: int32 [16, 2048, 2], P('section', 'expert'), may hold values from 0 to 7, all different within a row; in each aligned block of 128 rows (0 to 127, 128 to 255, ..., all dimensions but the last counted through in order) at most 48 rows name the same one
- gates_bwd: float32 [16, 2048, 2], P('section', 'expert'), may hold values from 0.2 to 1
- w_gate: bfloat16 [16, 16, 2560, 384], P('section', 'expert'), may hold values from -0.125 to 0.125
- w_up: bfloat16 [16, 16, 2560, 384], P('section', 'expert'), may hold values from -0.125 to 0.125
- w_down: bfloat16 [16, 16, 384, 2560], P('section', 'expert'), may hold values from -0.21875 to 0.21875
Outputs:
- forward_out: bfloat16 [16, 2048, 2560], P('section', 'expert')
- backward_out: bfloat16 [16, 2048, 2560], P('section', 'expert')
Inputs may be any that keep to these rules, and one draw needn't show every extreme that they name: `ids_fwd`: the 2 ids of a token differ. Among the 128 tokens of one device, no expert is chosen by more than 48, and some expert is chosen by exactly 48 in some device's tokens. `ids_bwd`: as ids_fwd.
All inputs are finite; a program needn't handle non-finite values.
Results may differ from a plain program's by a relative error of at most 0.014.
Values may be sent and summed in bfloat16 or wider, within the bound.
A program may use at most 128 MiB of HBM per device.

v0:
```python
import jax
import jax.numpy as jnp
from jax import lax
from jax.sharding import PartitionSpec as P

EXPERTS = 8
TOP = 2
CAP = 48


def passed_along(value, axis, steps):
    count = lax.axis_size(axis)
    pairs = [(source, (source + steps) % count) for source in range(count)]
    return lax.ppermute(value, axis, pairs)


def partner(value, axis, apart):
    mask = 2**apart
    pairs = [(source, source ^ mask) for source in range(lax.axis_size(axis))]
    return lax.ppermute(value, axis, pairs)


def slot_index(expert_ids):
    flat_ids = expert_ids.reshape(-1)
    onehot = (flat_ids[:, None] == jnp.arange(EXPERTS, dtype=jnp.int32)[None, :]).astype(jnp.int32)
    before = jnp.cumsum(onehot, axis=0) - onehot
    position = jnp.sum(before * onehot, axis=1)
    return flat_ids * CAP + position


def token_pairs(rows):
    width = rows.shape[1]
    return jnp.broadcast_to(rows[:, None, :], (rows.shape[0], TOP, width)).reshape(-1, width)


def pack_rows(pair_rows, slots, copies):
    width = pair_rows.shape[1]
    filled = jnp.zeros((EXPERTS * CAP, width), pair_rows.dtype).at[slots].set(pair_rows)
    widened = jnp.broadcast_to(
        filled.reshape(EXPERTS, 1, CAP, width), (EXPERTS, copies, CAP, width)
    )
    return widened.reshape(EXPERTS * copies, CAP, width)


def unpack_rows(returned, slots, copies):
    width = returned.shape[-1]
    summed = jnp.sum(returned.reshape(EXPERTS, copies, CAP, width).astype(jnp.float32), axis=1)
    return summed.reshape(EXPERTS * CAP, width)[slots].reshape(-1, TOP, width)


def expert_forward(rows, weight_g, weight_u, weight_d):
    gate_pre = jnp.dot(rows, weight_g, preferred_element_type=jnp.float32)
    up_pre = jnp.dot(rows, weight_u, preferred_element_type=jnp.float32)
    hidden = (jax.nn.silu(gate_pre) * up_pre).astype(jnp.bfloat16)
    return jnp.dot(hidden, weight_d, preferred_element_type=jnp.float32).astype(jnp.bfloat16)


def expert_backward(rows, grads, weight_g, weight_u, weight_d):
    contract = (((1,), (1,)), ((), ()))
    gate_pre = jnp.dot(rows, weight_g, preferred_element_type=jnp.float32)
    up_pre = jnp.dot(rows, weight_u, preferred_element_type=jnp.float32)
    sigma = jax.nn.sigmoid(gate_pre)
    hidden_grad = lax.dot_general(grads, weight_d, contract, preferred_element_type=jnp.float32)
    grad_gate = (hidden_grad * up_pre * sigma * (1.0 + gate_pre * (1.0 - sigma))).astype(
        jnp.bfloat16
    )
    grad_up = (hidden_grad * gate_pre * sigma).astype(jnp.bfloat16)
    back_gate = lax.dot_general(grad_gate, weight_g, contract, preferred_element_type=jnp.float32)
    back_up = lax.dot_general(grad_up, weight_u, contract, preferred_element_type=jnp.float32)
    return (back_gate + back_up).astype(jnp.bfloat16)


def on_device(
    handoff, grad_handoff, parked, ids_fwd, gates_fwd, ids_bwd, gates_bwd, w_gate, w_up, w_down
):
    arriving = passed_along(handoff[0], "section", 1)
    returning = passed_along(grad_handoff[0], "section", -1)
    top_bit = lax.axis_size("section").bit_length() - 2
    saved = partner(parked[0], "section", top_bit)
    copies = lax.axis_size("expert") // EXPERTS
    weight_g = w_gate[0, 0]
    weight_u = w_up[0, 0]
    weight_d = w_down[0, 0]
    width = arriving.shape[1]
    slots_f = slot_index(ids_fwd[0])
    slots_b = slot_index(ids_bwd[0])
    forward_slots = pack_rows(token_pairs(arriving), slots_f, copies)
    saved_slots = pack_rows(token_pairs(saved), slots_b, copies)
    scaled = (gates_bwd[0][:, :, None] * returning[:, None, :].astype(jnp.float32)).astype(
        jnp.bfloat16
    )
    grad_slots = pack_rows(scaled.reshape(-1, width), slots_b, copies)
    block = lax.all_to_all(forward_slots, "expert", split_axis=0, concat_axis=0, tiled=True)
    sources, count, _ = block.shape
    forward_ret = lax.all_to_all(
        expert_forward(block.reshape(-1, width), weight_g, weight_u, weight_d).reshape(
            sources, count, width
        ),
        "expert",
        split_axis=0,
        concat_axis=0,
        tiled=True,
    )
    block = lax.all_to_all(saved_slots, "expert", split_axis=0, concat_axis=0, tiled=True)
    sources, count, _ = block.shape
    result = expert_backward(
        block.reshape(-1, width),
        lax.all_to_all(grad_slots, "expert", split_axis=0, concat_axis=0, tiled=True).reshape(
            -1, width
        ),
        weight_g,
        weight_u,
        weight_d,
    )
    backward_ret = lax.all_to_all(
        result.reshape(sources, count, width), "expert", split_axis=0, concat_axis=0, tiled=True
    )
    picked_f = unpack_rows(forward_ret, slots_f, copies)
    forward_rows = jnp.sum(picked_f * gates_fwd[0][:, :, None], axis=1).astype(jnp.bfloat16)
    picked_b = unpack_rows(backward_ret, slots_b, copies)
    backward_rows = jnp.sum(picked_b, axis=1).astype(jnp.bfloat16)
    return (forward_rows[None], backward_rows[None])


def solution(mesh):
    return jax.shard_map(
        on_device,
        mesh=mesh,
        in_specs=(
            P("section", "expert", None),
            P("section", "expert", None),
            P("section", "expert", None),
            P("section", "expert", None),
            P("section", "expert", None),
            P("section", "expert", None),
            P("section", "expert", None),
            P("section", "expert", None, None),
            P("section", "expert", None, None),
            P("section", "expert", None, None),
        ),
        out_specs=(P("section", "expert", None), P("section", "expert", None)),
        check_vma=False,
    )
```

profile of v0, /device:TPU:99, one launch (start us, length us, event | category | flops | bytes accessed | tf_op | source)
XLA Modules:
  0.0 568.1 jit_solution(7691454618865857472)
XLA Ops:
  0.6 0.0 copy-start
  0.6 0.1 collective-permute-start.2
  0.7 0.9 copy.18
  1.7 0.1 eq.62
  1.8 0.1 eq.58
  1.9 0.6 reduce-window.16
  2.5 0.2 slice_reduce_fusion
  2.8 0.7 broadcast_multiply_fusion
  3.5 0.1 copy.17
  3.6 0.1 mul.94
  3.7 0.1 fusion.50
  3.8 12.8 %collective-permute-done.2 = bf16[128,2560]{1,0:T(8,128)(2,1)} collective-permute-done((bf16[128,2560]{1,0:T(8,128)(2,1)}, bf16[128,2560]{1,0:T(8,128)(2,1)}, u32[]{:S(2)}, u32[]{:S(2)}) %collective-permute-start.2) | collective-permute-done | bytes 655392 | tf_op jit(solution)/shard_map/ppermute | solution.py:20
  16.6 1.8 broadcast_in_dim.21
  18.4 1.4 reshape.228
  19.8 4.7 scatter_custom_fusion.2
  24.5 3.8 broadcast_in_dim.23
  28.3 9.4 %all-to-all-start.3 = ((bf16[16,48,2560]{2,1,0:T(8,128)(2,1)}), bf16[16,48,2560]{2,1,0:T(8,128)(2,1)}, u32[]{:S(2)}, u32[]{:S(2)}) async-start(bf16[16,48,2560]{2,1,0:T(8,128)(2,1)} %bitcast.92), calls=%async_computation.3 | async-start | bytes 7864320 | tf_op jit(solution)/shard_map/all_to_all | solution.py:104
  37.8 2.1 collective-permute-start.1
  39.9 0.1 copy.20
  40.0 0.1 mul.96
  40.1 9.7 %collective-permute-done.1 = bf16[128,2560]{1,0:T(8,128)(2,1)S(1)} collective-permute-done((bf16[128,2560]{1,0:T(8,128)(2,1)}, bf16[128,2560]{1,0:T(8,128)(2,1)S(1)}, u32[]{:S(2)}, u32[]{:S(2)}) %collective-permute-start.1) | collective-permute-done | bytes 655392 | tf_op jit(solution)/shard_map/ppermute | solution.py:14
  49.8 2.3 mul.98
  52.1 4.5 mul.99
  56.6 5.3 scatter_custom_fusion.1
  61.9 67.5 %all-to-all-done.3 = bf16[16,48,2560]{2,1,0:T(8,128)(2,1)} async-done(((bf16[16,48,2560]{2,1,0:T(8,128)(2,1)}), bf16[16,48,2560]{2,1,0:T(8,128)(2,1)}, u32[]{:S(2)}, u32[]{:S(2)}) %all-to-all-start.3) | async-done | bytes 3932192 | tf_op jit(solution)/shard_map/all_to_all | solution.py:104
  129.5 3.8 broadcast_in_dim.20
  133.3 7.2 %all-to-all-start.2 = ((bf16[16,48,2560]{2,1,0:T(8,128)(2,1)}), bf16[16,48,2560]{2,1,0:T(8,128)(2,1)}, u32[]{:S(2)}, u32[]{:S(2)}) async-start(bf16[16,48,2560]{2,1,0:T(8,128)(2,1)} %bitcast.91), calls=%async_computation.2 | async-start | bytes 7864320 | tf_op jit(solution)/shard_map/all_to_all | solution.py:108
  140.5 2.6 collective-permute-start
  143.2 0.1 copy.14
  143.3 0.1 eq.54
  143.4 0.1 eq.50
  143.6 0.6 reduce-window.14
  144.2 0.2 slice_reduce_fusion.1
  144.4 0.1 copy.13
  144.5 0.1 mul.86
  144.7 0.1 fusion.52
  144.8 5.9 %collective-permute-done = bf16[128,2560]{1,0:T(8,128)(2,1)} collective-permute-done((bf16[128,2560]{1,0:T(8,128)(2,1)S(1)}, bf16[128,2560]{1,0:T(8,128)(2,1)}, u32[]{:S(2)}, u32[]{:S(2)}) %collective-permute-start) | collective-permute-done | bytes 655392 | tf_op jit(solution)/shard_map/ppermute | solution.py:14
  150.7 1.8 broadcast_in_dim.16
  152.5 1.4 reshape.212
  153.9 4.8 scatter_custom_fusion
  158.7 72.1 %all-to-all-done.2 = bf16[16,48,2560]{2,1,0:T(8,128)(2,1)} async-done(((bf16[16,48,2560]{2,1,0:T(8,128)(2,1)}), bf16[16,48,2560]{2,1,0:T(8,128)(2,1)}, u32[]{:S(2)}, u32[]{:S(2)}) %all-to-all-start.2) | async-done | bytes 3932192 | tf_op jit(solution)/shard_map/all_to_all | solution.py:108
  230.8 3.8 broadcast_in_dim.18
  234.6 6.9 %all-to-all-start = ((bf16[16,48,2560]{2,1,0:T(8,128)(2,1)}), bf16[16,48,2560]{2,1,0:T(8,128)(2,1)}, u32[]{:S(2)}, u32[]{:S(2)}) async-start(bf16[16,48,2560]{2,1,0:T(8,128)(2,1)} %bitcast.93), calls=%async_computation | async-start | bytes 7864320 | tf_op jit(solution)/shard_map/all_to_all | solution.py:93
  241.5 5.1 fusion.10
  246.6 5.3 fusion
  251.9 10.5 %fusion.8 = f32[768,2560]{1,0:T(8,128)} fusion(bf16[1,1,2560,384]{3,2,1,0:T(8,128)(2,1)} %param.17, f32[768,384]{1,0:T(8,128)} %fusion, bf16[768,2560]{1,0:T(8,128)(2,1)} %bitcast.27, bf16[1,1,2560,384]{3,2,1,0:T(8,128)(2,1)S(1)} %copy-done, f32[768,384]{1,0:T(8,128)S(1)} %fusion.10), kind=kOutput, calls=%fused_computation.19 | convolution fusion | flops 3022848000 | bytes 18087936 | tf_op jit(solution)/shard_map/dot_general | solution.py:68
  262.4 7.8 %add_convert_fusion = bf16[768,2560]{1,0:T(8,128)(2,1)} fusion(f32[768,2560]{1,0:T(8,128)} %fusion.8, bf16[1,1,2560,384]{3,2,1,0:T(8,128)(2,1)S(1)} %copy-done, f32[768,384]{1,0:T(8,128)} %fusion, f32[768,384]{1,0:T(8,128)S(1)} %fusion.10), kind=kOutput, calls=%fused_computation.7 | convolution fusion | flops 1515651072 | bytes 16121856 | tf_op jit(solution)/shard_map/dot_general | solution.py:69
  270.3 60.0 %all-to-all-done = bf16[16,48,2560]{2,1,0:T(8,128)(2,1)} async-done(((bf16[16,48,2560]{2,1,0:T(8,128)(2,1)}), bf16[16,48,2560]{2,1,0:T(8,128)(2,1)}, u32[]{:S(2)}, u32[]{:S(2)}) %all-to-all-start) | async-done | bytes 3932192 | tf_op jit(solution)/shard_map/all_to_all | solution.py:93
  330.3 7.2 %all-to-all-start.4 = ((bf16[16,48,2560]{2,1,0:T(8,128)(2,1)}), bf16[16,48,2560]{2,1,0:T(8,128)(2,1)}, u32[]{:S(2)}, u32[]{:S(2)}) async-start(bf16[16,48,2560]{2,1,0:T(8,128)(2,1)} %bitcast.94), calls=%async_computation.4 | async-start | bytes 7864320 | tf_op jit(solution)/shard_map/all_to_all | solution.py:115
  337.5 4.9 fusion.12
  342.5 8.8 %convolution_convert_fusion = bf16[768,2560]{1,0:T(8,128)(2,1)} fusion(bf16[1,1,384,2560]{3,2,1,0:T(8,128)(2,1)} %param.19, bf16[768,2560]{1,0:T(8,128)(2,1)} %bitcast.7, bf16[1,1,2560,384]{3,2,1,0:T(8,128)(2,1)S(1)} %copy-done, f32[768,384]{1,0:T(8,128)S(1)} %fusion.12), kind=kOutput, calls=%fused_computation.8 | convolution fusion | flops 3023634432 | bytes 12976128 | tf_op jit(solution)/shard_map/dot_general | solution.py:55
  351.3 75.6 %all-to-all-done.4 = bf16[16,48,2560]{2,1,0:T(8,128)(2,1)} async-done(((bf16[16,48,2560]{2,1,0:T(8,128)(2,1)}), bf16[16,48,2560]{2,1,0:T(8,128)(2,1)}, u32[]{:S(2)}, u32[]{:S(2)}) %all-to-all-start.4) | async-done | bytes 3932192 | tf_op jit(solution)/shard_map/all_to_all | solution.py:115
  426.9 9.5 %all-to-all-start.1 = ((bf16[16,48,2560]{2,1,0:T(8,128)(2,1)}), bf16[16,48,2560]{2,1,0:T(8,128)(2,1)}, u32[]{:S(2)}, u32[]{:S(2)}) async-start(bf16[16,48,2560]{2,1,0:T(8,128)(2,1)} %bitcast.98), calls=%async_computation.1 | async-start | bytes 7864320 | tf_op jit(solution)/shard_map/all_to_all | solution.py:95
  436.4 0.1 copy.16
  436.6 5.2 convert_reduce_fusion
  441.8 6.3 %gather_fusion.1 = f32[256,2560]{1,0:T(8,128)} fusion(f32[384,2560]{1,0:T(8,128)} %bitcast.89, s32[1024]{0:T(1024)S(1)} %pad_clamp_fusion), kind=kCustom, calls=%fused_computation.1 | custom fusion | bytes 5243904 | tf_op jit(solution)/shard_map/gather | solution.py:48
  448.1 4.4 reshape.189
  452.4 87.1 %all-to-all-done.1 = bf16[16,48,2560]{2,1,0:T(8,128)(2,1)} async-done(((bf16[16,48,2560]{2,1,0:T(8,128)(2,1)}), bf16[16,48,2560]{2,1,0:T(8,128)(2,1)}, u32[]{:S(2)}, u32[]{:S(2)}) %all-to-all-start.1) | async-done | bytes 3932192 | tf_op jit(solution)/shard_map/all_to_all | solution.py:95
  539.5 5.1 convert_reduce_fusion.1
  544.6 6.2 %gather_fusion = f32[256,2560]{1,0:T(8,128)} fusion(f32[384,2560]{1,0:T(8,128)} %bitcast.90, s32[1024]{0:T(1024)S(1)} %pad_clamp_fusion.1), kind=kCustom, calls=%fused_computation | custom fusion | bytes 5243904 | tf_op jit(solution)/shard_map/gather | solution.py:48
  550.9 4.6 reshape.180
  555.5 0.0 copy-start.1
  555.5 5.9 %reduce_sum.65 = bf16[128,2560]{1,0:T(8,128)(2,1)} reduce(f32[128,2,2560]{2,1,0:T(2,128)} %reshape.189, f32[]{:T(128)} %constant.20.clone.1), dimensions={1}, to_apply=%region_12.13 | reduce | flops 327680 | bytes 3276804 | tf_op jit(solution)/shard_map/reduce_sum | solution.py:121
  561.4 6.3 %multiply_reduce_fusion = bf16[128,2560]{1,0:T(8,128)(2,1)} fusion(f32[128,2,2560]{2,1,0:T(2,128)} %reshape.180, f32[128,2]{1,0:T(8,128)S(1)} %copy.16), kind=kLoop, calls=%fused_computation.10 | loop fusion | flops 983040 | bytes 3277824 | tf_op jit(solution)/shard_map/reduce_sum | solution.py:119
  (23 shorter events, 0.1 us)
Async XLA Ops:
  0.6 251.3 %copy-start = (bf16[1,1,2560,384]{3,2,1,0:T(8,128)(2,1)S(1)}, bf16[1,1,2560,384]{3,2,1,0:T(8,128)(2,1)}, u32[]{:S(2)}) copy-start(bf16[1,1,2560,384]{3,2,1,0:T(8,128)(2,1)} %param.18) | copy-start | bytes 5898244
  0.6 16.0 %collective-permute-start.2 = (bf16[128,2560]{1,0:T(8,128)(2,1)}, bf16[128,2560]{1,0:T(8,128)(2,1)}, u32[]{:S(2)}, u32[]{:S(2)}) collective-permute-start(bf16[128,2560]{1,0:T(8,128)(2,1)} %bitcast.109), channel_id=1, source_target_pairs={{0,128},{16,144},{32,160},{48,176},{64,192},{80,208},{96,224},{112... | collective-permute-start | bytes 1966088 | tf_op jit(solution)/shard_map/ppermute | solution.py:20
  28.3 11.5 %copy-start.3 = (f32[1,128,2]{1,2,0:T(2,128)S(1)}, f32[1,128,2]{1,2,0:T(2,128)}, u32[]{:S(2)}) copy-start(f32[1,128,2]{1,2,0:T(2,128)} %param.16) | copy-start | bytes 3076
  28.3 101.1 %all-to-all-start.3 = ((bf16[16,48,2560]{2,1,0:T(8,128)(2,1)}), bf16[16,48,2560]{2,1,0:T(8,128)(2,1)}, u32[]{:S(2)}, u32[]{:S(2)}) async-start(bf16[16,48,2560]{2,1,0:T(8,128)(2,1)} %bitcast.92), calls=%async_computation.3 | async-start | bytes 7864320 | tf_op jit(solution)/shard_map/all_to_all | solution.py:104
  37.8 12.1 %collective-permute-start.1 = (bf16[128,2560]{1,0:T(8,128)(2,1)}, bf16[128,2560]{1,0:T(8,128)(2,1)S(1)}, u32[]{:S(2)}, u32[]{:S(2)}) collective-permute-start(bf16[128,2560]{1,0:T(8,128)(2,1)} %bitcast.110), channel_id=1, source_target_pairs={{0,240},{16,0},{32,16},{48,32},{64,48},{80,64},{96,80},{112,96},{1... | collective-permute-start | bytes 1966088 | tf_op jit(solution)/shard_map/ppermute | solution.py:14
  133.3 7.2 %copy-start.6 = (bf16[1,128,2560]{2,1,0:T(8,128)(2,1)S(1)}, bf16[1,128,2560]{2,1,0:T(8,128)(2,1)}, u32[]{:S(2)}) copy-start(bf16[1,128,2560]{2,1,0:T(8,128)(2,1)} %param.10) | copy-start | bytes 1966084
  133.3 9.9 %copy-start.2 = (s32[1,128,2]{1,2,0:T(2,128)S(1)}, s32[1,128,2]{1,2,0:T(2,128)}, u32[]{:S(2)}) copy-start(s32[1,128,2]{1,2,0:T(2,128)} %param.13) | copy-start | bytes 3076
  133.3 97.5 %all-to-all-start.2 = ((bf16[16,48,2560]{2,1,0:T(8,128)(2,1)}), bf16[16,48,2560]{2,1,0:T(8,128)(2,1)}, u32[]{:S(2)}, u32[]{:S(2)}) async-start(bf16[16,48,2560]{2,1,0:T(8,128)(2,1)} %bitcast.91), calls=%async_computation.2 | async-start | bytes 7864320 | tf_op jit(solution)/shard_map/all_to_all | solution.py:108
  140.5 10.2 %collective-permute-start = (bf16[128,2560]{1,0:T(8,128)(2,1)S(1)}, bf16[128,2560]{1,0:T(8,128)(2,1)}, u32[]{:S(2)}, u32[]{:S(2)}) collective-permute-start(bf16[128,2560]{1,0:T(8,128)(2,1)S(1)} %bitcast.111), channel_id=1, source_target_pairs={{0,16},{16,32},{32,48},{48,64},{64,80},{80,96},{96,112},{112,128},... | collective-permute-start | bytes 1966088 | tf_op jit(solution)/shard_map/ppermute | solution.py:14
  234.6 95.7 %all-to-all-start = ((bf16[16,48,2560]{2,1,0:T(8,128)(2,1)}), bf16[16,48,2560]{2,1,0:T(8,128)(2,1)}, u32[]{:S(2)}, u32[]{:S(2)}) async-start(bf16[16,48,2560]{2,1,0:T(8,128)(2,1)} %bitcast.93), calls=%async_computation | async-start | bytes 7864320 | tf_op jit(solution)/shard_map/all_to_all | solution.py:93
  241.5 5.1 copy-start.5
  330.3 96.7 %all-to-all-start.4 = ((bf16[16,48,2560]{2,1,0:T(8,128)(2,1)}), bf16[16,48,2560]{2,1,0:T(8,128)(2,1)}, u32[]{:S(2)}, u32[]{:S(2)}) async-start(bf16[16,48,2560]{2,1,0:T(8,128)(2,1)} %bitcast.94), calls=%async_computation.4 | async-start | bytes 7864320 | tf_op jit(solution)/shard_map/all_to_all | solution.py:115
  426.9 9.5 %copy-start.4 = (f32[1,128,2]{1,2,0:T(2,128)S(1)}, f32[1,128,2]{1,2,0:T(2,128)}, u32[]{:S(2)}) copy-start(f32[1,128,2]{1,2,0:T(2,128)} %param.14) | copy-start | bytes 3076
  426.9 112.6 %all-to-all-start.1 = ((bf16[16,48,2560]{2,1,0:T(8,128)(2,1)}), bf16[16,48,2560]{2,1,0:T(8,128)(2,1)}, u32[]{:S(2)}, u32[]{:S(2)}) async-start(bf16[16,48,2560]{2,1,0:T(8,128)(2,1)} %bitcast.98), calls=%async_computation.1 | async-start | bytes 7864320 | tf_op jit(solution)/shard_map/all_to_all | solution.py:95
  555.5 12.2 %copy-start.1 = (bf16[1,1,2560,384]{3,2,1,0:T(8,128)(2,1)S(1)}, bf16[1,1,2560,384]{3,2,1,0:T(8,128)(2,1)}, u32[]{:S(2)}) copy-start(bf16[1,1,2560,384]{3,2,1,0:T(8,128)(2,1)} %param.18) | copy-start | bytes 5898244
where the time goes:
time: 578 us; the launch traced here: 568 us
  waiting for transfers between devices  391 us (68%)
  local copies, waits for them, and re-layouts  58.5 us (10%)
  starting transfers between devices  45.1 us (8%)
  matrix products  42.5 us (7%)
  other arithmetic  30 us (5%)
    all_to_all x1, waiting for transfers between devices, on_device(): lax.all_to_all(expert_forward(block.reshape(-1, width), weight_g, weight_...  87.1 us
    all_to_all x1, waiting for transfers between devices, on_device(): lax.all_to_all(result.reshape(sources, count, width), 'expert', split_axi...  75.6 us
    all_to_all x1, waiting for transfers between devices, on_device(): lax.all_to_all(grad_slots, 'expert', split_axis=0, concat_axis=0, tiled=T...  72.1 us
    all_to_all x1, waiting for transfers between devices, on_device(): lax.all_to_all(saved_slots, 'expert', split_axis=0, concat_axis=0, tiled=...  67.5 us
    all_to_all x1, waiting for transfers between devices, on_device(): lax.all_to_all(forward_slots, 'expert', split_axis=0, concat_axis=0, tile...  60 us
    ppermute x2, waiting for transfers between devices, passed_along(): return lax.ppermute(value, axis, pairs)  15.6 us
    ppermute x1, waiting for transfers between devices, partner(): return lax.ppermute(value, axis, pairs)  12.8 us
    gather x2, local copies, waits for them, and re-layouts, unpack_rows(): return summed.reshape(EXPERTS * CAP, width)[slots].reshape(-1, TOP, width)  12.5 us
  transfers between devices with their start and end apart: 8, of which 8 were waited for; matrix products, arithmetic and copies ran while one was open for 15% of the time, Pallas kernels for 0%

commit v1 on v0

v1 whole, which is shorter than its diff:
```python
import jax
import jax.numpy as jnp
from jax import lax
from jax.experimental import pallas as pl
from jax.experimental.pallas import tpu as pltpu
from jax.sharding import PartitionSpec as P

EXPERTS = 8
CAP = 48
NY = 4
NZ = 4
TOK = 128
HALF = 64
D = 2560
HID = 384
ROWS = NY * CAP
NC = 512
STEPS = D // NC
F32 = jnp.float32
BF16 = jnp.bfloat16
NT = (((1,), (1,)), ((), ()))
N_COPIES = 93


def body(
    hand,
    grad,
    parked,
    meta,
    w_gate,
    w_up,
    w_down,
    out_f,
    out_b,
    wg,
    wu,
    wd,
    ids,
    pos_rows,
    gate_rows,
    pos_cols,
    gate_cols,
    x_s,
    x_r,
    x_f,
    in_s,
    in_r,
    in_f,
    stage,
    ret_b,
    ret_f,
    far,
    near,
    hop1,
    hop2,
    own_sum,
    acc_a,
    acc_u,
    acc_q,
    act_a,
    act_u,
    p_mat,
    q_mat,
    send_sem,
    recv_sem,
    local_sem,
):
    s = lax.axis_index("section")
    e = lax.axis_index("expert")
    y = e // NZ
    z = e % NZ
    zl = s // 8
    pair = z // 2

    def at(section, yy, zz):
        return (section, yy * NZ + zz)

    zp, zm, z2 = (z + 1) % 4, (z + 3) % 4, (z + 2) % 4
    nxt, prv, mate = (s + 1) % 16, (s + 15) % 16, (s + 8) % 16
    up_to = (z + zl) % 4
    down_to = (z + 3 + zl) % 4
    zp_dev, zm_dev, z2_dev = at(s, y, zp), at(s, y, zm), at(s, y, z2)
    y_dev = [None] + [at(s, (y + r) % 4, z) for r in (1, 2, 3)]

    counter = [0]
    pending = []

    def remote(src, dst, device):
        i = counter[0]
        counter[0] += 1
        copy = pltpu.make_async_remote_copy(
            src_ref=src,
            dst_ref=dst,
            send_sem=send_sem.at[i],
            recv_sem=recv_sem.at[i],
            device_id=device,
            device_id_type=pl.DeviceIdType.MESH,
        )
        pending.append(copy)
        return copy

    local = [
        pltpu.make_async_copy(w_gate.at[0, 0], wg, local_sem.at[0]),
        pltpu.make_async_copy(w_up.at[0, 0], wu, local_sem.at[1]),
        pltpu.make_async_copy(w_down.at[0, 0], wd, local_sem.at[2]),
    ]
    for copy in local:
        copy.start()
    ids[z] = meta[...]

    barrier = pltpu.get_barrier_semaphore()
    others = [at(nxt, y, z), at(prv, y, z), at(mate, y, up_to), at(mate, y, down_to)]
    others += [zp_dev, zm_dev, z2_dev] + y_dev[1:]
    for device in others:
        pl.semaphore_signal(barrier, inc=1, device_id=device, device_id_type=pl.DeviceIdType.MESH)
    pl.semaphore_wait(barrier, len(others))

    meta_copies = [remote(ids.at[z], ids.at[z], device) for device in (zp_dev, zm_dev, z2_dev)]
    for copy in meta_copies:
        copy.start()
    halves = (pl.ds(0, HALF), pl.ds(HALF, HALF))
    s_up = [remote(parked.at[0, h], x_s.at[z, h], at(mate, y, up_to)) for h in halves]
    s_down = [remote(parked.at[0, h], x_s.at[z, h], at(mate, y, down_to)) for h in halves]
    shift_r = remote(grad.at[0], x_r.at[z], at(prv, y, z))
    shift_f = remote(hand.at[0], x_f.at[z], at(nxt, y, z))
    shift_r.start()
    shift_f.start()
    for one, two in zip(s_up, s_down):
        one.start()
        two.start()

    for copy in meta_copies:
        copy.wait_recv()
    lower = lax.broadcasted_iota(jnp.int32, (TOK, TOK), 0) < lax.broadcasted_iota(
        jnp.int32, (TOK, TOK), 1
    )
    lower = lower.astype(F32).astype(BF16)
    expert_row = lax.broadcasted_iota(jnp.int32, (EXPERTS, TOK), 0).astype(F32)
    filler = jnp.zeros((TOK - EXPERTS, TOK), F32)
    for zz in range(NZ):
        for which in range(2):
            base = 4 * which
            first = ids[zz, base : base + 1, :] == expert_row
            second = ids[zz, base + 1 : base + 2, :] == expert_row
            named = jnp.where(first | second, 1.0, 0.0)
            before = jnp.dot(named.astype(BF16), lower, preferred_element_type=F32)
            place = jnp.where(named > 0.5, before, -1.0)
            gate = jnp.where(first, ids[zz, base + 2 : base + 3, :], 0.0) + jnp.where(
                second, ids[zz, base + 3 : base + 4, :], 0.0
            )
            pos_rows[which, zz] = place
            gate_rows[which, zz] = gate
            pos_cols[which, zz] = jnp.concatenate([place, filler], axis=0).T
            gate_cols[which, zz] = jnp.concatenate([gate, filler], axis=0).T

    experts = [((y + r) % 4) * 2 + pair for r in range(NY)]
    slot_row = lax.broadcasted_iota(jnp.int32, (CAP, TOK), 0).astype(F32)
    own_rows = pl.ds(pl.multiple_of(y * CAP, 16), CAP)

    def columns(i):
        return pl.ds(pl.multiple_of(i * NC, NC), NC)

    def pack(which, zz, source, target, slot, scaled):
        picks = []
        gates = []
        for r in range(NY):
            one = jnp.where(slot_row == pos_rows[which, zz, pl.ds(experts[r], 1), :], 1.0, 0.0)
            picks.append(one)
            if scaled:
                gates.append(
                    jnp.sum(one * gate_rows[which, zz, pl.ds(experts[r], 1), :], axis=1, keepdims=True)
                )
        p_mat[...] = jnp.concatenate(picks, axis=0).astype(BF16)
        gate = jnp.concatenate(gates, axis=0) if scaled else None

        @pl.loop(0, STEPS)
        def _(i):
            c = columns(i)
            rows = jnp.dot(p_mat[...], source[zz, :, c], preferred_element_type=F32)
            if scaled:
                rows = rows * gate
            rows = rows.astype(BF16)
            target[zz, own_rows, c] = rows[:CAP]
            stage[slot, :, c] = rows[CAP:]

        copies = []
        for r in (1, 2, 3):
            copy = remote(
                stage.at[slot, pl.ds((r - 1) * CAP, CAP)], target.at[zz, own_rows], y_dev[r]
            )
            copy.start()
            copies.append(copy)
        return copies

    def forward(zz):
        acc_a[...] = jnp.zeros_like(acc_a)
        acc_u[...] = jnp.zeros_like(acc_u)

        @pl.loop(0, STEPS)
        def _(i):
            c = columns(i)
            rows = in_f[zz, :, c]
            acc_a[...] += jnp.dot(rows, wg[c, :], preferred_element_type=F32)
            acc_u[...] += jnp.dot(rows, wu[c, :], preferred_element_type=F32)

        a = acc_a[...]
        act_a[...] = (a / (1.0 + jnp.exp(-a)) * acc_u[...]).astype(BF16)

        @pl.loop(0, STEPS)
        def _(i):
            c = columns(i)
            in_f[zz, :, c] = jnp.dot(act_a[...], wd[:, c], preferred_element_type=F32).astype(BF16)

    def backward(zz):
        acc_a[...] = jnp.zeros_like(acc_a)
        acc_u[...] = jnp.zeros_like(acc_u)
        acc_q[...] = jnp.zeros_like(acc_q)

        @pl.loop(0, STEPS)
        def _(i):
            c = columns(i)
            rows = in_s[zz, :, c]
            acc_a[...] += jnp.dot(rows, wg[c, :], preferred_element_type=F32)
            acc_u[...] += jnp.dot(rows, wu[c, :], preferred_element_type=F32)
            acc_q[...] += lax.dot_general(in_r[zz, :, c], wd[:, c], NT, preferred_element_type=F32)

        a = acc_a[...]
        q = acc_q[...]
        sigma = 1.0 / (1.0 + jnp.exp(-a))
        act_a[...] = (q * acc_u[...] * sigma * (1.0 + a * (1.0 - sigma))).astype(BF16)
        act_u[...] = (q * a * sigma).astype(BF16)

        @pl.loop(0, STEPS)
        def _(i):
            c = columns(i)
            back = lax.dot_general(act_a[...], wg[c, :], NT, preferred_element_type=F32)
            back += lax.dot_general(act_u[...], wu[c, :], NT, preferred_element_type=F32)
            in_r[zz, :, c] = back.astype(BF16)

    def send_back(zz, result, returned):
        copies = []
        for r in (1, 2, 3):
            rows = pl.ds(pl.multiple_of(((y + r) % 4) * CAP, 16), CAP)
            copy = remote(
                result.at[zz, rows], returned.at[zz, pl.ds((4 - r) * CAP, CAP)], y_dev[r]
            )
            copy.start()
            copies.append(copy)
        returned[zz, pl.ds(0, CAP), :] = result[zz, own_rows, :]
        return copies

    lane = lax.broadcasted_iota(jnp.int32, (TOK, ROWS), 1)
    block = jnp.where(lane >= CAP, 1, 0) + jnp.where(lane >= 2 * CAP, 1, 0)
    block = block + jnp.where(lane >= 3 * CAP, 1, 0)
    slot_col = (lane - block * CAP).astype(F32)
    expert_lane = lax.broadcasted_iota(jnp.int32, (TOK, TOK), 1)

    def spread(table, which, zz):
        cols = table[which, zz]
        wide = jnp.zeros((TOK, ROWS), F32)
        for r in range(NY):
            one = jnp.sum(jnp.where(expert_lane == experts[r], cols, 0.0), axis=1, keepdims=True)
            wide = wide + jnp.where(block == r, one, 0.0)
        return wide

    def combine(which, zz, returned, store):
        weight = jnp.where(spread(pos_cols, which, zz) == slot_col, 1.0, 0.0)
        if which == 0:
            weight = weight * spread(gate_cols, which, zz)
            high = weight.astype(BF16)
            p_low = (weight - high.astype(F32)).astype(BF16)
            q_mat[0] = high
            q_mat[1] = p_low
        else:
            q_mat[0] = weight.astype(BF16)

        @pl.loop(0, STEPS)
        def _(i):
            c = columns(i)
            total = jnp.dot(q_mat[0], returned[zz, :, c], preferred_element_type=F32)
            if which == 0:
                total += jnp.dot(q_mat[1], returned[zz, :, c], preferred_element_type=F32)
            store(c, total)

    def landed(copies):
        for copy in copies:
            copy.wait_recv()

    def to_far(which, returned):
        def store(c, total):
            far[which, :, c] = total.astype(BF16)

        combine(which, z2, returned, store)
        up = remote(far.at[which, halves[0]], hop1.at[which, 0], zp_dev)
        down = remote(far.at[which, halves[1]], hop1.at[which, 1], zm_dev)
        up.start()
        down.start()
        return up, down

    def to_near(which, returned, direction, arriving):
        zz = zp if direction == 0 else zm
        device = zp_dev if direction == 0 else zm_dev
        through, free = halves[direction], halves[1 - direction]

        def store(c, total):
            near[which, direction, :, c] = total.astype(BF16)

        combine(which, zz, returned, store)
        first = remote(near.at[which, direction, free], hop2.at[which, direction, free], device)
        first.start()
        arriving.wait_recv()
        near[which, direction, through, :] = (
            near[which, direction, through, :].astype(F32) + hop1[which, direction].astype(F32)
        ).astype(BF16)
        second = remote(
            near.at[which, direction, through], hop2.at[which, direction, through], device
        )
        second.start()
        return [first, second]

    def to_own(which, returned):
        def store(c, total):
            own_sum[which, :, c] = total

        combine(which, z, returned, store)

    def finish(which, out):
        out[0] = (
            own_sum[which] + hop2[which, 0].astype(F32) + hop2[which, 1].astype(F32)
        ).astype(BF16)

    def spread_first(x):
        return [
            remote(x.at[z], x.at[z], zp_dev),
            remote(x.at[z], x.at[z], zm_dev),
        ]

    def spread_second(x):
        return [
            remote(x.at[zm, halves[0]], x.at[zm, halves[0]], zp_dev),
            remote(x.at[zp, halves[1]], x.at[zp, halves[1]], zm_dev),
        ]

    def start(copies):
        for copy in copies:
            copy.start()

    zs_up, zs_down = (z + 3 + zl) % 4, (z + zl) % 4
    zs_up2, zs_down2 = (z + 2 + zl) % 4, (z + 1 + zl) % 4

    shift_r.wait_recv()
    got_r_own = pack(1, z, x_r, in_r, 0, True)
    shift_f.wait_recv()
    got_f_own = pack(0, z, x_f, in_f, 1, False)

    s_up2 = [remote(x_s.at[zs_up, h], x_s.at[zs_up, h], zp_dev) for h in halves]
    s_down2 = [remote(x_s.at[zs_down, h], x_s.at[zs_down, h], zm_dev) for h in halves]
    for i in range(2):
        s_up[i].wait_recv()
        s_up2[i].start()
        s_down[i].wait_recv()
        s_down2[i].start()

    got_s = [pack(1, zs_up, x_s, in_s, 2, False), pack(1, zs_down, x_s, in_s, 3, False)]
    r_first = spread_first(x_r)
    start(r_first)

    for copy in local:
        copy.wait()
    landed(got_f_own)
    forward(z)

    landed(s_up2)
    got_s.append(pack(1, zs_up2, x_s, in_s, 4, False))
    landed(s_down2)
    got_s.append(pack(1, zs_down2, x_s, in_s, 5, False))

    landed(r_first)
    r_second = spread_second(x_r)
    start(r_second)
    f_first = spread_first(x_f)
    start(f_first)
    got_r_m = pack(1, zm, x_r, in_r, 6, True)
    got_r_p = pack(1, zp, x_r, in_r, 7, True)

    landed(got_r_own)
    for copies in got_s:
        landed(copies)
    backward(z)

    landed(r_second)
    got_r_2 = pack(1, z2, x_r, in_r, 8, True)
    back_own = send_back(z, in_r, ret_b)
    landed(got_r_m)
    backward(zm)
    landed(got_r_p)
    backward(zp)
    landed(f_first)
    f_second = spread_second(x_f)
    start(f_second)
    landed(got_r_2)
    backward(z2)
    back_2 = send_back(z2, in_r, ret_b)
    back_p = send_back(zp, in_r, ret_b)
    back_m = send_back(zm, in_r, ret_b)
    got_f_m = pack(0, zm, x_f, in_f, 9, False)
    got_f_p = pack(0, zp, x_f, in_f, 10, False)
    landed(f_second)
    got_f_2 = pack(0, z2, x_f, in_f, 11, False)
    landed(back_2)
    b_up, b_down = to_far(1, ret_b)
    landed(back_p)
    b_near = to_near(1, ret_b, 0, b_up)
    landed(back_m)
    b_near += to_near(1, ret_b, 1, b_down)
    landed(back_own)
    to_own(1, ret_b)

    landed(got_f_m)
    forward(zm)
    landed(got_f_p)
    forward(zp)
    landed(got_f_2)
    forward(z2)
    fore_2 = send_back(z2, in_f, ret_f)
    fore_p = send_back(zp, in_f, ret_f)
    fore_m = send_back(zm, in_f, ret_f)
    fore_own = send_back(z, in_f, ret_f)
    landed(b_near)
    finish(1, out_b)
    landed(fore_2)
    f_up, f_down = to_far(0, ret_f)
    landed(fore_p)
    f_near = to_near(0, ret_f, 0, f_up)
    landed(fore_m)
    f_near += to_near(0, ret_f, 1, f_down)
    landed(fore_own)
    to_own(0, ret_f)
    landed(f_near)
    finish(0, out_f)

    for copy in pending:
        copy.wait_send()
    assert counter[0] == N_COPIES, counter[0]


def on_device(
    handoff, grad_handoff, parked, ids_fwd, gates_fwd, ids_bwd, gates_bwd, w_gate, w_up, w_down
):
    meta = jnp.concatenate(
        [ids_fwd[0].astype(F32), gates_fwd[0], ids_bwd[0].astype(F32), gates_bwd[0]], axis=1
    ).T
    anywhere = pl.BlockSpec(memory_space=pl.ANY)
    vmem = pl.BlockSpec(memory_space=pltpu.VMEM)
    result = jax.ShapeDtypeStruct((1, TOK, D), BF16)
    return pl.pallas_call(
        body,
        out_shape=(result, result),
        in_specs=[anywhere] * 3 + [vmem] + [anywhere] * 3,
        out_specs=(vmem, vmem),
        scratch_shapes=[
            pltpu.VMEM((D, HID), BF16),
            pltpu.VMEM((D, HID), BF16),
            pltpu.VMEM((HID, D), BF16),
            pltpu.VMEM((NZ, 8, TOK), F32),
            pltpu.VMEM((2, NZ, EXPERTS, TOK), F32),
            pltpu.VMEM((2, NZ, EXPERTS, TOK), F32),
            pltpu.VMEM((2, NZ, TOK, TOK), F32),
            pltpu.VMEM((2, NZ, TOK, TOK), F32),
            pltpu.VMEM((NZ, TOK, D), BF16),
            pltpu.VMEM((NZ, TOK, D), BF16),
            pltpu.VMEM((NZ, TOK, D), BF16),
            pltpu.VMEM((NZ, ROWS, D), BF16),
            pltpu.VMEM((NZ, ROWS, D), BF16),
            pltpu.VMEM((NZ, ROWS, D), BF16),
            pltpu.VMEM((12, ROWS - CAP, D), BF16),
            pltpu.VMEM((NZ, ROWS, D), BF16),
            pltpu.VMEM((NZ, ROWS, D), BF16),
            pltpu.VMEM((2, TOK, D), BF16),
            pltpu.VMEM((2, 2, TOK, D), BF16),
            pltpu.VMEM((2, 2, HALF, D), BF16),
            pltpu.VMEM((2, 2, TOK, D), BF16),
            pltpu.VMEM((2, TOK, D), F32),
            pltpu.VMEM((ROWS, HID), F32),
            pltpu.VMEM((ROWS, HID), F32),
            pltpu.VMEM((ROWS, HID), F32),
            pltpu.VMEM((ROWS, HID), BF16),
            pltpu.VMEM((ROWS, HID), BF16),
            pltpu.VMEM((ROWS, TOK), BF16),
            pltpu.VMEM((2, TOK, ROWS), BF16),
            pltpu.SemaphoreType.DMA((N_COPIES,)),
            pltpu.SemaphoreType.DMA((N_COPIES,)),
            pltpu.SemaphoreType.DMA((3,)),
        ],
        compiler_params=pltpu.CompilerParams(
            collective_id=0, has_side_effects=True, vmem_limit_bytes=62 * 2**20
        ),
        name="relay_experts",
    )(handoff, grad_handoff, parked, meta, w_gate, w_up, w_down)


def solution(mesh):
    rows = P("section", "expert", None)
    weights = P("section", "expert", None, None)
    return jax.shard_map(
        on_device,
        mesh=mesh,
        in_specs=(rows,) * 7 + (weights,) * 3,
        out_specs=(rows, rows),
        check_vma=False,
    )
```

time: 578 us -> 273 us (0.47)
  the two profiles are of different devices: /device:TPU:99 before, /device:TPU:58 now
where the time goes in v1:
time: 273 us
  Pallas kernels  267 us (98%)
  local copies, waits for them, and re-layouts  3.93 us (1%)
    pallas_call x1, Pallas kernels, on_device(): pl.pallas_call(body, out_shape=(result, result), in_specs=[anywhere] * 3...  267 us

profile of v1, /device:TPU:58, one launch (start us, length us, event | category | flops | bytes accessed | tf_op | source)
XLA Modules:
  0.0 273.1 jit_solution(17451051726423734629)
XLA Ops:
  0.6 0.7 convert_bitcast_fusion
  1.3 1.3 maximum_bitcast_fusion.meta
  2.6 266.5 %relay_experts.1 = (bf16[1,128,2560]{2,1,0:T(8,128)(2,1)}, bf16[1,128,2560]{2,1,0:T(8,128)(2,1)}) custom-call(bf16[1,128,2560]{2,1,0:T(8,128)(2,1)} %hand.1, bf16[1,128,2560]{2,1,0:T(8,128)(2,1)} %grad.1, bf16[1,128,2560]{2,1,0:T(8,128)(2,1)} %parked.1, f32[8,128]{1,0:T(8,128)} %maximum_bitcast_fusion.meta, bf16[1,1,2560,384]{3,2,1,0:T(8,128)(2,1)} %w_gate.1, ...), custom_call_target="tpu_custom_call" | custom-call | tf_op jit(solution)/shard_map/relay_experts/pallas_call | solution.py:456
  269.2 2.0 copy.14
  271.1 2.0 copy.15

commit v2 on v1

--- a/solution.py
+++ b/solution.py
@@ -15,11 +15,12 @@
 HID = 384
 ROWS = NY * CAP
 NC = 512
+PACK = 640
 STEPS = D // NC
 F32 = jnp.float32
 BF16 = jnp.bfloat16
 NT = (((1,), (1,)), ((), ()))
-N_COPIES = 93
+N_COPIES = 115
 
 
 def body(
@@ -30,8 +31,7 @@
     w_gate,
     w_up,
     w_down,
-    out_f,
-    out_b,
+    out,
     wg,
     wu,
     wd,
@@ -108,40 +108,20 @@
         copy.start()
     ids[z] = meta[...]
 
-    barrier = pltpu.get_barrier_semaphore()
-    others = [at(nxt, y, z), at(prv, y, z), at(mate, y, up_to), at(mate, y, down_to)]
-    others += [zp_dev, zm_dev, z2_dev] + y_dev[1:]
-    for device in others:
-        pl.semaphore_signal(barrier, inc=1, device_id=device, device_id_type=pl.DeviceIdType.MESH)
-    pl.semaphore_wait(barrier, len(others))
-
-    meta_copies = [remote(ids.at[z], ids.at[z], device) for device in (zp_dev, zm_dev, z2_dev)]
-    for copy in meta_copies:
-        copy.start()
-    halves = (pl.ds(0, HALF), pl.ds(HALF, HALF))
-    s_up = [remote(parked.at[0, h], x_s.at[z, h], at(mate, y, up_to)) for h in halves]
-    s_down = [remote(parked.at[0, h], x_s.at[z, h], at(mate, y, down_to)) for h in halves]
-    shift_r = remote(grad.at[0], x_r.at[z], at(prv, y, z))
-    shift_f = remote(hand.at[0], x_f.at[z], at(nxt, y, z))
-    shift_r.start()
-    shift_f.start()
-    for one, two in zip(s_up, s_down):
-        one.start()
-        two.start()
-
-    for copy in meta_copies:
-        copy.wait_recv()
     lower = lax.broadcasted_iota(jnp.int32, (TOK, TOK), 0) < lax.broadcasted_iota(
         jnp.int32, (TOK, TOK), 1
     )
     lower = lower.astype(F32).astype(BF16)
     expert_row = lax.broadcasted_iota(jnp.int32, (EXPERTS, TOK), 0).astype(F32)
     filler = jnp.zeros((TOK - EXPERTS, TOK), F32)
-    for zz in range(NZ):
+
+    def tables(zz):
         for which in range(2):
             base = 4 * which
-            first = ids[zz, base : base + 1, :] == expert_row
-            second = ids[zz, base + 1 : base + 2, :] == expert_row
+            one = ids[zz, base : base + 1, :]
+            two = ids[zz, base + 1 : base + 2, :]
+            first = one == expert_row
+            second = two == expert_row
             named = jnp.where(first | second, 1.0, 0.0)
             before = jnp.dot(named.astype(BF16), lower, preferred_element_type=F32)
             place = jnp.where(named > 0.5, before, -1.0)
@@ -153,6 +133,32 @@
             pos_cols[which, zz] = jnp.concatenate([place, filler], axis=0).T
             gate_cols[which, zz] = jnp.concatenate([gate, filler], axis=0).T
 
+    barrier = pltpu.get_barrier_semaphore()
+    others = [at(nxt, y, z), at(prv, y, z), at(mate, y, up_to), at(mate, y, down_to)]
+    others += [zp_dev, zm_dev, z2_dev] + y_dev[1:]
+    for device in others:
+        pl.semaphore_signal(barrier, inc=1, device_id=device, device_id_type=pl.DeviceIdType.MESH)
+    tables(z)
+    pl.semaphore_wait(barrier, len(others))
+
+    meta_copies = [remote(ids.at[z], ids.at[z], device) for device in (zp_dev, zm_dev, z2_dev)]
+    for copy in meta_copies:
+        copy.start()
+    halves = (pl.ds(0, HALF), pl.ds(HALF, HALF))
+    s_up = [remote(parked.at[0, h], x_s.at[z, h], at(mate, y, up_to)) for h in halves]
+    s_down = [remote(parked.at[0, h], x_s.at[z, h], at(mate, y, down_to)) for h in halves]
+    wide = (pl.ds(0, D // 2), pl.ds(D // 2, D // 2))
+    shift = [
+        [remote(hand.at[0, :, c], x_f.at[z, :, c], at(nxt, y, z)) for c in wide],
+        [remote(grad.at[0, :, c], x_r.at[z, :, c], at(prv, y, z)) for c in wide],
+    ]
+    for i in range(2):
+        shift[1][i].start()
+        shift[0][i].start()
+    for one, two in zip(s_up, s_down):
+        one.start()
+        two.start()
+
     experts = [((y + r) % 4) * 2 + pair for r in range(NY)]
     slot_row = lax.broadcasted_iota(jnp.int32, (CAP, TOK), 0).astype(F32)
     own_rows = pl.ds(pl.multiple_of(y * CAP, 16), CAP)
@@ -160,7 +166,7 @@
     def columns(i):
         return pl.ds(pl.multiple_of(i * NC, NC), NC)
 
-    def pack(which, zz, source, target, slot, scaled):
+    def sort_rows(which, zz, source, target, slot, scaled):
         picks = []
         gates = []
         for r in range(NY):
@@ -173,23 +179,34 @@
         p_mat[...] = jnp.concatenate(picks, axis=0).astype(BF16)
         gate = jnp.concatenate(gates, axis=0) if scaled else None
 
-        @pl.loop(0, STEPS)
-        def _(i):
-            c = columns(i)
-            rows = jnp.dot(p_mat[...], source[zz, :, c], preferred_element_type=F32)
-            if scaled:
-                rows = rows * gate
-            rows = rows.astype(BF16)
-            target[zz, own_rows, c] = rows[:CAP]
-            stage[slot, :, c] = rows[CAP:]
-
-        copies = []
-        for r in (1, 2, 3):
-            copy = remote(
-                stage.at[slot, pl.ds((r - 1) * CAP, CAP)], target.at[zz, own_rows], y_dev[r]
+        def some(first, last):
+            @pl.loop(first, last)
+            def _(i):
+                c = pl.ds(pl.multiple_of(i * PACK, PACK), PACK)
+                rows = jnp.dot(p_mat[...], source[zz, :, c], preferred_element_type=F32)
+                if scaled:
+                    rows = rows * gate
+                rows = rows.astype(BF16)
+                target[zz, own_rows, c] = rows[:CAP]
+                stage[slot, :, c] = rows[CAP:]
+
+        return some
+
+    def along_y(zz, target, slot, c):
+        return [
+            remote(
+                stage.at[slot, pl.ds((r - 1) * CAP, CAP), c],
+                target.at[zz, own_rows, c],
+                y_dev[r],
             )
+            for r in (1, 2, 3)
+        ]
+
+    def pack(which, zz, source, target, slot, scaled):
+        sort_rows(which, zz, source, target, slot, scaled)(0, D // PACK)
+        copies = along_y(zz, target, slot, pl.ds(0, D))
+        for copy in copies:
             copy.start()
-            copies.append(copy)
         return copies
 
     def forward(zz):
@@ -237,16 +254,16 @@
             back += lax.dot_general(act_u[...], wu[c, :], NT, preferred_element_type=F32)
             in_r[zz, :, c] = back.astype(BF16)
 
-    def send_back(zz, result, returned):
+    def send_back(zz, result, returned, c=pl.ds(0, D)):
         copies = []
         for r in (1, 2, 3):
             rows = pl.ds(pl.multiple_of(((y + r) % 4) * CAP, 16), CAP)
             copy = remote(
-                result.at[zz, rows], returned.at[zz, pl.ds((4 - r) * CAP, CAP)], y_dev[r]
+                result.at[zz, rows, c], returned.at[zz, pl.ds((4 - r) * CAP, CAP), c], y_dev[r]
             )
             copy.start()
             copies.append(copy)
-        returned[zz, pl.ds(0, CAP), :] = result[zz, own_rows, :]
+        returned[zz, pl.ds(0, CAP), c] = result[zz, own_rows, c]
         return copies
 
     lane = lax.broadcasted_iota(jnp.int32, (TOK, ROWS), 1)
@@ -263,7 +280,7 @@
             wide = wide + jnp.where(block == r, one, 0.0)
         return wide
 
-    def combine(which, zz, returned, store):
+    def combine(which, zz, returned, store, first=0, last=D // PACK):
         weight = jnp.where(spread(pos_cols, which, zz) == slot_col, 1.0, 0.0)
         if which == 0:
             weight = weight * spread(gate_cols, which, zz)
@@ -274,9 +291,9 @@
         else:
             q_mat[0] = weight.astype(BF16)
 
-        @pl.loop(0, STEPS)
+        @pl.loop(first, last)
         def _(i):
-            c = columns(i)
+            c = pl.ds(pl.multiple_of(i * PACK, PACK), PACK)
             total = jnp.dot(q_mat[0], returned[zz, :, c], preferred_element_type=F32)
             if which == 0:
                 total += jnp.dot(q_mat[1], returned[zz, :, c], preferred_element_type=F32)
@@ -297,7 +314,7 @@
         down.start()
         return up, down
 
-    def to_near(which, returned, direction, arriving):
+    def to_near(which, returned, direction, arriving, parts):
         zz = zp if direction == 0 else zm
         device = zp_dev if direction == 0 else zm_dev
         through, free = halves[direction], halves[1 - direction]
@@ -305,18 +322,28 @@
         def store(c, total):
             near[which, direction, :, c] = total.astype(BF16)
 
-        combine(which, zz, returned, store)
-        first = remote(near.at[which, direction, free], hop2.at[which, direction, free], device)
-        first.start()
-        arriving.wait_recv()
-        near[which, direction, through, :] = (
-            near[which, direction, through, :].astype(F32) + hop1[which, direction].astype(F32)
-        ).astype(BF16)
-        second = remote(
-            near.at[which, direction, through], hop2.at[which, direction, through], device
-        )
-        second.start()
-        return [first, second]
+        copies = []
+        for i, part in enumerate(parts):
+            landed(part)
+            steps = D // PACK // len(parts)
+            c = pl.ds(i * steps * PACK, steps * PACK)
+            combine(which, zz, returned, store, i * steps, (i + 1) * steps)
+            first = remote(
+                near.at[which, direction, free, c], hop2.at[which, direction, free, c], device
+            )
+            first.start()
+            if i == 0:
+                arriving.wait_recv()
+            near[which, direction, through, c] = (
+                near[which, direction, through, c].astype(F32)
+                + hop1[which, direction, :, c].astype(F32)
+            ).astype(BF16)
+            second = remote(
+                near.at[which, direction, through, c], hop2.at[which, direction, through, c], device
+            )
+            second.start()
+            copies += [first, second]
+        return copies
 
     def to_own(which, returned):
         def store(c, total):
@@ -325,14 +352,15 @@
         combine(which, z, returned, store)
 
     def finish(which, out):
-        out[0] = (
+        out[which] = (
             own_sum[which] + hop2[which, 0].astype(F32) + hop2[which, 1].astype(F32)
         ).astype(BF16)
 
-    def spread_first(x):
+    def spread_first(x, through):
+        one, two = (halves[0], halves[1]) if through else (halves[1], halves[0])
         return [
-            remote(x.at[z], x.at[z], zp_dev),
-            remote(x.at[z], x.at[z], zm_dev),
+            remote(x.at[z, one], x.at[z, one], zp_dev),
+            remote(x.at[z, two], x.at[z, two], zm_dev),
         ]
 
     def spread_second(x):
@@ -341,6 +369,13 @@
             remote(x.at[zp, halves[1]], x.at[zp, halves[1]], zm_dev),
         ]
 
+    def nearby(copies):
+        copies[0].wait_recv()
+        copies[2].wait_recv()
+
+    def straight(copies):
+        copies[1].wait_recv()
+
     def start(copies):
         for copy in copies:
             copy.start()
@@ -348,100 +383,135 @@
     zs_up, zs_down = (z + 3 + zl) % 4, (z + zl) % 4
     zs_up2, zs_down2 = (z + 2 + zl) % 4, (z + 1 + zl) % 4
 
-    shift_r.wait_recv()
-    got_r_own = pack(1, z, x_r, in_r, 0, True)
-    shift_f.wait_recv()
-    got_f_own = pack(0, z, x_f, in_f, 1, False)
+    own = [
+        [along_y(z, in_f, 0, c) for c in wide],
+        [along_y(z, in_r, 1, c) for c in wide],
+    ]
+    got_f_own, got_r_own = own[0][0] + own[0][1], own[1][0] + own[1][1]
+
+    def own_rows_out(which):
+        some = sort_rows(which, z, (x_f, x_r)[which], (in_f, in_r)[which], which, which == 1)
+        for i in range(2):
+            shift[which][i].wait_recv()
+            some(i * D // PACK // 2, (i + 1) * D // PACK // 2)
+            start(own[which][i])
 
     s_up2 = [remote(x_s.at[zs_up, h], x_s.at[zs_up, h], zp_dev) for h in halves]
     s_down2 = [remote(x_s.at[zs_down, h], x_s.at[zs_down, h], zm_dev) for h in halves]
+
+    odd = s % 2 == 1
+
+    @pl.when(odd)
+    def _():
+        own_rows_out(0)
+
+    @pl.when(jnp.logical_not(odd))
+    def _():
+        own_rows_out(1)
+
+    for copy in meta_copies:
+        copy.wait_recv()
+    for zz in (zp, zm, z2):
+        tables(zz)
+
     for i in range(2):
         s_up[i].wait_recv()
         s_up2[i].start()
         s_down[i].wait_recv()
         s_down2[i].start()
 
+    @pl.when(odd)
+    def _():
+        own_rows_out(1)
+
+    @pl.when(jnp.logical_not(odd))
+    def _():
+        own_rows_out(0)
+
     got_s = [pack(1, zs_up, x_s, in_s, 2, False), pack(1, zs_down, x_s, in_s, 3, False)]
-    r_first = spread_first(x_r)
-    start(r_first)
-
     for copy in local:
         copy.wait()
+
+    r_first_a, r_first_b = spread_first(x_r, True), spread_first(x_r, False)
+    f_first_a, f_first_b = spread_first(x_f, True), spread_first(x_f, False)
+    r_second, f_second = spread_second(x_r), spread_second(x_f)
+
+    landed([s_up2[0], s_down2[0]])
+    start(r_first_a)
     landed(got_f_own)
     forward(z)
-
-    landed(s_up2)
+    landed([s_up2[1], s_down2[1]])
+    start(r_first_b)
     got_s.append(pack(1, zs_up2, x_s, in_s, 4, False))
-    landed(s_down2)
     got_s.append(pack(1, zs_down2, x_s, in_s, 5, False))
-
-    landed(r_first)
-    r_second = spread_second(x_r)
+    fore_own = send_back(z, in_f, ret_f)
+
+    landed(r_first_a)
     start(r_second)
-    f_first = spread_first(x_f)
-    start(f_first)
-    got_r_m = pack(1, zm, x_r, in_r, 6, True)
-    got_r_p = pack(1, zp, x_r, in_r, 7, True)
-
+    landed(r_first_b)
+    start(f_first_a)
+    got_r_p = pack(1, zp, x_r, in_r, 6, True)
+    got_r_m = pack(1, zm, x_r, in_r, 7, True)
     landed(got_r_own)
     for copies in got_s:
         landed(copies)
     backward(z)
-
     landed(r_second)
+    start(f_first_b)
     got_r_2 = pack(1, z2, x_r, in_r, 8, True)
-    back_own = send_back(z, in_r, ret_b)
-    landed(got_r_m)
-    backward(zm)
     landed(got_r_p)
     backward(zp)
-    landed(f_first)
-    f_second = spread_second(x_f)
+    back_p = send_back(zp, in_r, ret_b)
+    landed(f_first_a)
     start(f_second)
     landed(got_r_2)
     backward(z2)
     back_2 = send_back(z2, in_r, ret_b)
-    back_p = send_back(zp, in_r, ret_b)
+    landed(got_r_m)
+    backward(zm)
+    landed(f_first_b)
+    nearby(back_2)
     back_m = send_back(zm, in_r, ret_b)
-    got_f_m = pack(0, zm, x_f, in_f, 9, False)
+    straight(back_2)
+    b_up, b_down = to_far(1, ret_b)
+    landed(f_second)
+    got_f_2 = pack(0, z2, x_f, in_f, 9, False)
+    b_near = to_near(1, ret_b, 0, b_up, [back_p])
     got_f_p = pack(0, zp, x_f, in_f, 10, False)
-    landed(f_second)
-    got_f_2 = pack(0, z2, x_f, in_f, 11, False)
-    landed(back_2)
-    b_up, b_down = to_far(1, ret_b)
-    landed(back_p)
-    b_near = to_near(1, ret_b, 0, b_up)
-    landed(back_m)
-    b_near += to_near(1, ret_b, 1, b_down)
-    landed(back_own)
-    to_own(1, ret_b)
-
-    landed(got_f_m)
-    forward(zm)
-    landed(got_f_p)
-    forward(zp)
+    b_near += to_near(1, ret_b, 1, b_down, [back_m])
     landed(got_f_2)
     forward(z2)
     fore_2 = send_back(z2, in_f, ret_f)
-    fore_p = send_back(zp, in_f, ret_f)
-    fore_m = send_back(zm, in_f, ret_f)
-    fore_own = send_back(z, in_f, ret_f)
-    landed(b_near)
-    finish(1, out_b)
-    landed(fore_2)
+    got_f_m = pack(0, zm, x_f, in_f, 11, False)
+    landed(got_f_p)
+    forward(zp)
+    nearby(fore_2)
+    fore_p = [send_back(zp, in_f, ret_f, c) for c in wide]
+    straight(fore_2)
     f_up, f_down = to_far(0, ret_f)
-    landed(fore_p)
-    f_near = to_near(0, ret_f, 0, f_up)
-    landed(fore_m)
-    f_near += to_near(0, ret_f, 1, f_down)
+    landed(got_f_m)
+    forward(zm)
+    fore_m = [send_back(zm, in_f, ret_f, c) for c in wide]
     landed(fore_own)
     to_own(0, ret_f)
+    f_near = to_near(0, ret_f, 0, f_up, fore_p)
+    back_own = send_back(z, in_r, ret_b)
+    f_near += to_near(0, ret_f, 1, f_down, fore_m)
+    landed(back_own)
+    to_own(1, ret_b)
+    landed(b_near)
+    finish(1, out)
     landed(f_near)
-    finish(0, out_f)
+    finish(0, out)
 
     for copy in pending:
         copy.wait_send()
     assert counter[0] == N_COPIES, counter[0]
+
+
+def part_ways(both, out_f, out_b):
+    out_f[0] = both[0]
+    out_b[0] = both[1]
 
 
 def on_device(
@@ -452,12 +522,11 @@
     ).T
     anywhere = pl.BlockSpec(memory_space=pl.ANY)
     vmem = pl.BlockSpec(memory_space=pltpu.VMEM)
-    result = jax.ShapeDtypeStruct((1, TOK, D), BF16)
-    return pl.pallas_call(
+    both = pl.pallas_call(
         body,
-        out_shape=(result, result),
+        out_shape=jax.ShapeDtypeStruct((2, TOK, D), BF16),
         in_specs=[anywhere] * 3 + [vmem] + [anywhere] * 3,
-        out_specs=(vmem, vmem),
+        out_specs=vmem,
         scratch_shapes=[
             pltpu.VMEM((D, HID), BF16),
             pltpu.VMEM((D, HID), BF16),
@@ -498,6 +567,15 @@
         name="relay_experts",
     )(handoff, grad_handoff, parked, meta, w_gate, w_up, w_down)
 
+    result = jax.ShapeDtypeStruct((1, TOK, D), BF16)
+    return pl.pallas_call(
+        part_ways,
+        out_shape=(result, result),
+        in_specs=[vmem],
+        out_specs=(vmem, vmem),
+        name="part_ways",
+    )(both)
+
 
 def solution(mesh):
     rows = P("section", "expert", None)

time: 273 us -> 260 us (0.952); the launches traced: 273 us -> 256 us
  Pallas kernels: 267 us -> 254 us
  local copies, waits for them, and re-layouts: 3.93 us -> 0 us
    pallas_call x1 -> x2, Pallas kernels: 267 us -> 254 us  [the longest x1 251 us: on_device(): pl.pallas_call(body, out_shape=jax.ShapeDtypeStruct((2, TOK, D), BF16), i...]
    unnamed x2 -> x0, local copies, waits for them, and re-layouts: 3.93 us -> none
where the time goes in v2:
time: 260 us; the launch traced here: 256 us
  Pallas kernels  254 us (98%)
    pallas_call x1, Pallas kernels, on_device(): pl.pallas_call(body, out_shape=jax.ShapeDtypeStruct((2, TOK, D), BF16), i...  251 us

profile of v2, /device:TPU:58, one launch (start us, length us, event | category | flops | bytes accessed | tf_op | source)
XLA Modules:
  0.0 256.3 jit_solution(6919742413666536956)
XLA Ops:
  0.6 0.7 convert_bitcast_fusion
  1.3 1.3 maximum_bitcast_fusion.meta
  2.6 251.3 %relay_experts.1.both = bf16[2,128,2560]{2,1,0:T(8,128)(2,1)} custom-call(bf16[1,128,2560]{2,1,0:T(8,128)(2,1)} %hand.1, bf16[1,128,2560]{2,1,0:T(8,128)(2,1)} %grad.1, bf16[1,128,2560]{2,1,0:T(8,128)(2,1)} %parked.1, f32[8,128]{1,0:T(8,128)} %maximum_bitcast_fusion.meta, bf16[1,1,2560,384]{3,2,1,0:T(8,128)(2,1)} %w_gate.1, bf16[1,1,2560,384]{3,2,1,0:T(8,128)(2,1)} %w_up.1, ...), custom_call_target="tpu_custom_call" | custom-call | tf_op jit(solution)/shard_map/relay_experts/pallas_call | solution.py:525
  253.9 2.4 part_ways.1

commit v3 on v2

--- a/solution.py
+++ b/solution.py
@@ -21,13 +21,17 @@
 BF16 = jnp.bfloat16
 NT = (((1,), (1,)), ((), ()))
 N_COPIES = 115
+LAST_PARTS = 2
 
 
 def body(
     hand,
     grad,
     parked,
-    meta,
+    ids_f,
+    gates_f,
+    ids_b,
+    gates_b,
     w_gate,
     w_up,
     w_down,
@@ -106,7 +110,10 @@
     ]
     for copy in local:
         copy.start()
-    ids[z] = meta[...]
+    ids[z, 0:2, :] = ids_f[...].astype(F32)
+    ids[z, 2:4, :] = gates_f[...]
+    ids[z, 4:6, :] = ids_b[...].astype(F32)
+    ids[z, 6:8, :] = gates_b[...]
 
     lower = lax.broadcasted_iota(jnp.int32, (TOK, TOK), 0) < lax.broadcasted_iota(
         jnp.int32, (TOK, TOK), 1
@@ -314,7 +321,7 @@
         down.start()
         return up, down
 
-    def to_near(which, returned, direction, arriving, parts):
+    def to_near(which, returned, direction, arriving, back, part=0, parts=1):
         zz = zp if direction == 0 else zm
         device = zp_dev if direction == 0 else zm_dev
         through, free = halves[direction], halves[1 - direction]
@@ -322,28 +329,25 @@
         def store(c, total):
             near[which, direction, :, c] = total.astype(BF16)
 
-        copies = []
-        for i, part in enumerate(parts):
-            landed(part)
-            steps = D // PACK // len(parts)
-            c = pl.ds(i * steps * PACK, steps * PACK)
-            combine(which, zz, returned, store, i * steps, (i + 1) * steps)
-            first = remote(
-                near.at[which, direction, free, c], hop2.at[which, direction, free, c], device
-            )
-            first.start()
-            if i == 0:
-                arriving.wait_recv()
-            near[which, direction, through, c] = (
-                near[which, direction, through, c].astype(F32)
-                + hop1[which, direction, :, c].astype(F32)
-            ).astype(BF16)
-            second = remote(
-                near.at[which, direction, through, c], hop2.at[which, direction, through, c], device
-            )
-            second.start()
-            copies += [first, second]
-        return copies
+        landed(back)
+        steps = D // PACK // parts
+        c = pl.ds(part * steps * PACK, steps * PACK)
+        combine(which, zz, returned, store, part * steps, (part + 1) * steps)
+        first = remote(
+            near.at[which, direction, free, c], hop2.at[which, direction, free, c], device
+        )
+        first.start()
+        if part == 0:
+            arriving.wait_recv()
+        near[which, direction, through, c] = (
+            near[which, direction, through, c].astype(F32)
+            + hop1[which, direction, :, c].astype(F32)
+        ).astype(BF16)
+        second = remote(
+            near.at[which, direction, through, c], hop2.at[which, direction, through, c], device
+        )
+        second.start()
+        return [first, second]
 
     def to_own(which, returned):
         def store(c, total):
@@ -379,6 +383,8 @@
     def start(copies):
         for copy in copies:
             copy.start()
+
+    strips = [pl.ds(i * D // LAST_PARTS, D // LAST_PARTS) for i in range(LAST_PARTS)]
 
     zs_up, zs_down = (z + 3 + zl) % 4, (z + zl) % 4
     zs_up2, zs_down2 = (z + 2 + zl) % 4, (z + 1 + zl) % 4
@@ -476,9 +482,9 @@
     b_up, b_down = to_far(1, ret_b)
     landed(f_second)
     got_f_2 = pack(0, z2, x_f, in_f, 9, False)
-    b_near = to_near(1, ret_b, 0, b_up, [back_p])
+    b_near = to_near(1, ret_b, 0, b_up, back_p)
     got_f_p = pack(0, zp, x_f, in_f, 10, False)
-    b_near += to_near(1, ret_b, 1, b_down, [back_m])
+    b_near += to_near(1, ret_b, 1, b_down, back_m)
     landed(got_f_2)
     forward(z2)
     fore_2 = send_back(z2, in_f, ret_f)
@@ -486,17 +492,23 @@
     landed(got_f_p)
     forward(zp)
     nearby(fore_2)
-    fore_p = [send_back(zp, in_f, ret_f, c) for c in wide]
+    fore_p = [send_back(zp, in_f, ret_f, strips[0])]
     straight(fore_2)
     f_up, f_down = to_far(0, ret_f)
     landed(got_f_m)
     forward(zm)
-    fore_m = [send_back(zm, in_f, ret_f, c) for c in wide]
+    fore_m = [send_back(zm, in_f, ret_f, strips[0])]
+    for c in strips[1:]:
+        fore_p.append(send_back(zp, in_f, ret_f, c))
+        fore_m.append(send_back(zm, in_f, ret_f, c))
     landed(fore_own)
     to_own(0, ret_f)
-    f_near = to_near(0, ret_f, 0, f_up, fore_p)
-    back_own = send_back(z, in_r, ret_b)
-    f_near += to_near(0, ret_f, 1, f_down, fore_m)
+    f_near = []
+    for i in range(LAST_PARTS):
+        f_near += to_near(0, ret_f, 0, f_up, fore_p[i], i, LAST_PARTS)
+        f_near += to_near(0, ret_f, 1, f_down, fore_m[i], i, LAST_PARTS)
+        if i == 0:
+            back_own = send_back(z, in_r, ret_b)
     landed(back_own)
     to_own(1, ret_b)
     landed(b_near)
@@ -517,15 +529,13 @@
 def on_device(
     handoff, grad_handoff, parked, ids_fwd, gates_fwd, ids_bwd, gates_bwd, w_gate, w_up, w_down
 ):
-    meta = jnp.concatenate(
-        [ids_fwd[0].astype(F32), gates_fwd[0], ids_bwd[0].astype(F32), gates_bwd[0]], axis=1
-    ).T
+    meta = [ids_fwd[0].T, gates_fwd[0].T, ids_bwd[0].T, gates_bwd[0].T]
     anywhere = pl.BlockSpec(memory_space=pl.ANY)
     vmem = pl.BlockSpec(memory_space=pltpu.VMEM)
     both = pl.pallas_call(
         body,
         out_shape=jax.ShapeDtypeStruct((2, TOK, D), BF16),
-        in_specs=[anywhere] * 3 + [vmem] + [anywhere] * 3,
+        in_specs=[anywhere] * 3 + [vmem] * 4 + [anywhere] * 3,
         out_specs=vmem,
         scratch_shapes=[
             pltpu.VMEM((D, HID), BF16),
@@ -565,7 +575,7 @@
             collective_id=0, has_side_effects=True, vmem_limit_bytes=62 * 2**20
         ),
         name="relay_experts",
-    )(handoff, grad_handoff, parked, meta, w_gate, w_up, w_down)
+    )(handoff, grad_handoff, parked, *meta, w_gate, w_up, w_down)
 
     result = jax.ShapeDtypeStruct((1, TOK, D), BF16)
     return pl.pallas_call(

time: 260 us -> 258 us (level)
  no operation moved by 1% of the time
where the time goes in v3:
time: 258 us; the launch traced here: 254 us
  Pallas kernels  253 us (98%)
    pallas_call x1, Pallas kernels, on_device(): pl.pallas_call(body, out_shape=jax.ShapeDtypeStruct((2, TOK, D), BF16), i...  251 us

profile of v3, /device:TPU:58, one launch (start us, length us, event | category | flops | bytes accessed | tf_op | source)
XLA Modules:
  0.0 253.6 jit_solution(11621307565833062965)
XLA Ops:
  0.6 250.5 %relay_experts.1.both = bf16[2,128,2560]{2,1,0:T(8,128)(2,1)} custom-call(bf16[1,128,2560]{2,1,0:T(8,128)(2,1)} %hand.1, bf16[1,128,2560]{2,1,0:T(8,128)(2,1)} %grad.1, bf16[1,128,2560]{2,1,0:T(8,128)(2,1)} %parked.1, s32[2,128]{1,0:T(2,128)} %bitcast.12, f32[2,128]{1,0:T(2,128)} %bitcast.13, s32[2,128]{1,0:T(2,128)} %bitcast.14, f32[2,128]{1,0:T(2,128)} %bitcast.15, ...), custom_call_target="tpu_custom_call" | custom-call | tf_op jit(solution)/shard_map/relay_experts/pallas_call | solution.py:535
  251.1 2.4 part_ways.1
